TPU v7x, 128 devices: a whole 4x4x4 slice. The times are simulated.
128 devices in a mesh: rows: 32 (over y, z, core), mp: 4 (over x).
Axes of the slice: x: 4, y: 4, z: 4, core: 2. Of those that a mesh axis runs over, the one named last changes fastest.
Arguments:
- calib: bfloat16 [2048, 8192], P('rows', 'mp'), may hold values from -40 to 40
- weight: bfloat16 [8192, 8192], P('rows', 'mp'), may hold values from -6 to 6
- inverse_factor: float32 [8192, 8192], P('rows', 'mp'), may hold values from -10 to 12, as said below
- pruned_blocks: int32 [7], replicated, may hold values from 0 to 63, as said below
Outputs:
- pruned_weight: bfloat16 [8192, 8192], P('rows', 'mp')
- next_gram: float32 [8192, 8192], P('rows', 'mp')
Inputs may be any that keep to these rules, and one draw needn't show every extreme that they name: `pruned_blocks`: 7 distinct block numbers in any order; block b holds rows b * 128 to b * 128 + 127. `inverse_factor`: symmetric and positive definite.
All inputs are finite; a program needn't handle non-finite values.
Results may differ from a plain program's by a relative error of at most 0.0095.
Values may be sent and summed in bfloat16 or wider, within the bound.
No kernel may reach another device: no remote copies, remote signals or barrier semaphores. Data moves between devices by JAX's collectives and lax.ppermute only.
A program may use at most 128 MiB of HBM per device.

v0:
```python
import jax
import jax.numpy as jnp
from jax import lax
from jax.sharding import PartitionSpec as P

BLOCK = 128


def spd_solve(chol_lower, right_side):
    forward = lax.linalg.triangular_solve(chol_lower, right_side, left_side=True, lower=True)
    return lax.linalg.triangular_solve(
        chol_lower, forward, left_side=True, lower=True, transpose_a=True
    )


def shards(calib, weight, inverse_factor, pruned_blocks):
    rows_dev = weight.shape[0]
    width_dev = weight.shape[1]
    full_width = width_dev * lax.axis_size("mp")
    row_start = lax.axis_index("rows") * rows_dev
    col_start = lax.axis_index("mp") * width_dev
    starts = pruned_blocks * BLOCK
    block_count = pruned_blocks.shape[0]
    col_pieces = []
    for slot_index in range(block_count):
        offset = starts[slot_index] - col_start
        inside = ((offset >= 0) & (offset < width_dev)).astype(jnp.float32)
        clamped = jnp.clip(offset, 0, width_dev - BLOCK)
        col_pieces.append(lax.dynamic_slice_in_dim(inverse_factor, clamped, BLOCK, 1) * inside)
    columns = lax.psum(jnp.concatenate(col_pieces, axis=1), "mp")
    weight_parts = []
    inverse_parts = []
    for slot_index in range(block_count):
        offset = starts[slot_index] - row_start
        inside = ((offset >= 0) & (offset < rows_dev)).astype(jnp.float32)
        clamped = jnp.clip(offset, 0, rows_dev - BLOCK)
        weight_parts.append(
            lax.dynamic_slice_in_dim(weight, clamped, BLOCK, 0).astype(jnp.float32) * inside
        )
        inverse_parts.append(lax.dynamic_slice_in_dim(columns, clamped, BLOCK, 0) * inside)
    kept_rows = lax.psum(jnp.concatenate(weight_parts, axis=0).astype(jnp.bfloat16), "rows").astype(
        jnp.float32
    )
    inverse_square = lax.psum(jnp.concatenate(inverse_parts, axis=0), "rows")
    chol_lower = jnp.linalg.cholesky(inverse_square)
    solved = spd_solve(chol_lower, kept_rows)
    update = jnp.dot(columns, solved, precision=lax.Precision.HIGHEST)
    block_ids = (row_start + jnp.arange(rows_dev, dtype=jnp.int32)) // BLOCK
    kept_mask = 1.0 - jnp.any(block_ids[:, None] == pruned_blocks[None, :], axis=1).astype(
        jnp.float32
    )
    pruned_weight = ((weight.astype(jnp.float32) - update) * kept_mask[:, None]).astype(
        jnp.bfloat16
    )
    out_scale = float(full_width) ** (-0.5)
    partial_value = lax.dot_general(
        lax.all_gather(calib, "rows", axis=0, tiled=True),
        pruned_weight,
        (((1,), (1,)), ((), ())),
        preferred_element_type=jnp.float32,
    )
    token_count = partial_value.shape[0]
    own_rows = (
        lax.psum_scatter(partial_value, "mp", scatter_dimension=0, tiled=True) * out_scale
    ).astype(jnp.bfloat16)
    gram_term = lax.dot_general(
        own_rows,
        lax.all_gather(own_rows, "rows", axis=1, tiled=True),
        (((0,), (0,)), ((), ())),
        preferred_element_type=jnp.float32,
    )
    gram_block = (
        lax.psum_scatter(
            gram_term.astype(jnp.bfloat16), "mp", scatter_dimension=1, tiled=True
        ).astype(jnp.float32)
        / token_count
    )
    return (pruned_weight, gram_block)


def solution(mesh):
    return jax.shard_map(
        shards,
        mesh=mesh,
        in_specs=(P("rows", "mp"), P("rows", "mp"), P("rows", "mp"), P()),
        out_specs=(P("rows", "mp"), P("rows", "mp")),
        check_vma=False,
    )
```

profile of v0, /device:TPU:1, one launch (start us, length us, event | category | flops | bytes accessed | tf_op | source)
XLA Modules:
  0.0 788.2 jit_solution(16158695444413011221)
XLA Ops:
  13.4 1.8 constant_dynamic-slice_fusion.1
  28.4 35.7 %all-reduce.5.cloned.1.call-done = f32[256,896]{0,1:T(8,128)} async-done(((f32[256,896]{0,1:T(8,128)}), f32[256,896]{0,1:T(8,128)}) %all-reduce.5.cloned.1.call-update) | async-done | bytes 917520 | tf_op jit(solution)/shard_map/psum | solution.py:30
  64.1 1.3 multiply_dynamic-update-slice_fusion.6
  65.4 1.4 multiply_dynamic-update-slice_fusion.5
  66.7 1.4 multiply_dynamic-update-slice_fusion.4
  70.0 1.7 copy-done.7
  72.5 108.5 %all-reduce.9.cloned.1.call-done = bf16[896,2048]{1,0:T(8,128)(2,1)} async-done(((bf16[896,2048]{1,0:T(8,128)(2,1)}), bf16[896,2048]{1,0:T(8,128)(2,1)}) %all-reduce.9.cloned.1.call-update) | async-done | bytes 3670032 | tf_op jit(solution)/shard_map/psum | solution.py:41
  181.0 6.0 convert_element_type.111
  187.0 106.7 %all-reduce.7.cloned.1.call-done = f32[896,896]{0,1:T(8,128)} async-done(((f32[896,896]{0,1:T(8,128)}), f32[896,896]{0,1:T(8,128)}) %all-reduce.7.cloned.1.call-update) | async-done | bytes 3211280 | tf_op jit(solution)/shard_map/psum | solution.py:44
  293.7 5.0 copy.21
  298.7 2.2 fusion.16
  301.0 1.7 copy-done.6
  302.7 11.7 %cholesky.195 = f32[128,128]{1,0:T(8,128)S(1)} custom-call(f32[128,128]{1,0:T(8,128)S(1)} %cholesky.502), custom_call_target="Cholesky" | custom-call | tf_op jit(solution)/shard_map/jit(cholesky)/cholesky | solution.py:45
  314.6 9.8 %custom-call.56 = f32[1,128,128]{1,2,0:T(8,128)S(1)} custom-call(f32[1,128,128]{2,1,0:T(8,128)S(1)} %get-tuple-element.55), custom_call_target="InvertDiagBlocksLowerTriangular" | custom-call | tf_op jit(solution)/shard_map/jit(cholesky)/cholesky | solution.py:45
  324.5 1.5 constant_dynamic-update-slice_fusion.28
  325.9 1.5 convolution_subtract_fusion.9
  328.2 11.7 %cholesky.216 = f32[128,128]{1,0:T(8,128)S(1)} custom-call(f32[128,128]{1,0:T(8,128)S(1)} %cholesky.506), custom_call_target="Cholesky" | custom-call | tf_op jit(solution)/shard_map/jit(cholesky)/cholesky | solution.py:45
  340.7 10.0 %custom-call.57 = f32[1,128,128]{1,2,0:T(8,128)S(1)} custom-call(f32[1,128,128]{2,1,0:T(8,128)S(1)} %get-tuple-element.52), custom_call_target="InvertDiagBlocksLowerTriangular" | custom-call | tf_op jit(solution)/shard_map/jit(cholesky)/cholesky | solution.py:45
  350.6 1.4 convolution_dynamic-update-slice_fusion.1
  352.0 1.7 convolution_subtract_fusion.10
  354.3 13.2 %cholesky.411 = f32[128,128]{1,0:T(8,128)} custom-call(f32[128,128]{1,0:T(8,128)} %cholesky.511), custom_call_target="Cholesky" | custom-call | tf_op jit(solution)/shard_map/jit(cholesky)/cholesky | solution.py:45
  367.5 1.5 select_reduce_fusion.4
  369.0 11.3 %custom-call.58 = f32[1,128,128]{1,2,0:T(8,128)} custom-call(f32[1,128,128]{2,1,0:T(8,128)} %get-tuple-element.49), custom_call_target="InvertDiagBlocksLowerTriangular" | custom-call | tf_op jit(solution)/shard_map/jit(cholesky)/cholesky | solution.py:45
  381.5 1.7 convolution_subtract_fusion.11
  383.8 12.9 %cholesky.430 = f32[128,128]{1,0:T(8,128)S(1)} custom-call(f32[128,128]{1,0:T(8,128)} %cholesky.516), custom_call_target="Cholesky" | custom-call | tf_op jit(solution)/shard_map/jit(cholesky)/cholesky | solution.py:45
  397.4 10.6 %custom-call.59 = f32[1,128,128]{1,2,0:T(8,128)S(1)} custom-call(f32[1,128,128]{2,1,0:T(8,128)} %get-tuple-element.46), custom_call_target="InvertDiagBlocksLowerTriangular" | custom-call | tf_op jit(solution)/shard_map/jit(cholesky)/cholesky | solution.py:45
  408.4 1.7 convolution_subtract_fusion.12
  410.1 11.7 %cholesky.449 = f32[128,128]{1,0:T(8,128)S(1)} custom-call(f32[128,128]{1,0:T(8,128)S(1)} %cholesky.521), custom_call_target="Cholesky" | custom-call | tf_op jit(solution)/shard_map/jit(cholesky)/cholesky | solution.py:45
  422.4 9.8 %custom-call.60 = f32[1,128,128]{1,2,0:T(8,128)S(1)} custom-call(f32[1,128,128]{2,1,0:T(8,128)S(1)} %get-tuple-element.43), custom_call_target="InvertDiagBlocksLowerTriangular" | custom-call | tf_op jit(solution)/shard_map/jit(cholesky)/cholesky | solution.py:45
  432.5 1.6 convolution_subtract_fusion.13
  434.1 11.9 %cholesky.469 = f32[128,128]{1,0:T(8,128)S(1)} custom-call(f32[128,128]{1,0:T(8,128)S(1)} %cholesky.526), custom_call_target="Cholesky" | custom-call | tf_op jit(solution)/shard_map/jit(cholesky)/cholesky | solution.py:45
  446.0 9.8 %custom-call.61 = f32[1,128,128]{1,2,0:T(8,128)S(1)} custom-call(f32[1,128,128]{2,1,0:T(8,128)S(1)} %get-tuple-element.40), custom_call_target="InvertDiagBlocksLowerTriangular" | custom-call | tf_op jit(solution)/shard_map/jit(cholesky)/cholesky | solution.py:45
  456.0 1.3 convolution_subtract_fusion.14
  458.0 11.7 %cholesky.487 = f32[128,128]{1,0:T(8,128)S(1)} custom-call(f32[128,128]{1,0:T(8,128)S(1)} %convolution_subtract_fusion.14), custom_call_target="Cholesky" | custom-call | tf_op jit(solution)/shard_map/jit(cholesky)/cholesky | solution.py:45
  473.6 1.3 compare_reduce_fusion.3
  478.1 2.0 select_select_fusion
  480.1 24.9 %while.1 = (s32[]{:T(128)}, f32[896,896]{1,0:T(8,128)}, s32[7,2]{0,1:T(2,128)S(1)}, f32[7,128,128]{2,1,0:T(8,128)}, s32[]{:T(128)}) while((s32[]{:T(128)}, f32[896,896]{1,0:T(8,128)}, s32[7,2]{0,1:T(2,128)S(1)}, f32[7,128,128]{2,1,0:T(8,128)}, s32[]{:T(128)}) %tuple.62), condition=%wide.while_cond, body=%wide.while_body.sunk | while | flops 2 | bytes 132705 | solution.py:11
  480.7 2.9 bitcast_dynamic-update-slice_fusion.2
  484.3 2.9 bitcast_dynamic-update-slice_fusion.2
  487.8 2.9 bitcast_dynamic-update-slice_fusion.2
  491.4 2.9 bitcast_dynamic-update-slice_fusion.2
  495.0 2.9 bitcast_dynamic-update-slice_fusion.2
  498.5 2.9 bitcast_dynamic-update-slice_fusion.2
  502.1 2.8 bitcast_dynamic-update-slice_fusion.2
  504.9 70.7 %custom-call.62 = f32[7,128,128]{1,2,0:T(8,128)} custom-call(f32[7,128,128]{2,1,0:T(8,128)} %get-tuple-element.9), custom_call_target="InvertDiagBlocksLowerTriangular" | custom-call | tf_op jit(solution)/shard_map/triangular_solve | solution.py:11
  575.7 1.8 constant_dynamic-update-slice_fusion.4
  577.6 2.4 convolution_subtract_fusion.8
  581.1 2.6 convolution_subtract_fusion.6
  584.9 2.0 fusion.34
  588.1 2.4 fusion.40
  591.5 3.3 convolution_subtract_fusion.5
  595.9 3.4 convolution_subtract_fusion.2
  606.1 2.1 fusion.31
  609.2 2.3 fusion.37
  612.9 3.1 convolution_subtract_fusion.3
  617.6 3.8 convolution_subtract_fusion.1
  624.2 7.1 fusion.30
  631.4 7.6 convolution_bitcast_fusion
  639.1 29.3 %reduce-scatter.3.cloned.1.call-done = f32[512,256]{0,1:T(8,128)} async-done(((f32[2048,256]{0,1:T(8,128)}), f32[512,256]{0,1:T(8,128)}) %reduce-scatter.3.cloned.1.call-update) | async-done | bytes 524304 | tf_op jit(solution)/shard_map/reduce_scatter | solution.py:64
  668.4 1.8 multiply_convert_fusion.7
  670.2 54.3 %all-gather.5.cloned.1.call-done = bf16[512,8192]{0,1:T(8,128)(2,1)} async-done(((bf16[512,256]{0,1:T(8,128)(2,1)}), bf16[512,8192]{0,1:T(8,128)(2,1)}) %all-gather.5.cloned.1.call-update) | async-done | bytes 8388624 | tf_op jit(solution)/shard_map/all_gather | solution.py:68
  724.5 7.8 convolution_convert_fusion
  732.4 46.1 %reduce-scatter.5.cloned.1.call-done = bf16[256,2048]{1,0:T(8,128)(2,1)} async-done(((bf16[256,8192]{1,0:T(8,128)(2,1)}), bf16[256,2048]{1,0:T(8,128)(2,1)}) %reduce-scatter.5.cloned.1.call-update) | async-done | bytes 1048592 | tf_op jit(solution)/shard_map/reduce_scatter | solution.py:73
  778.4 2.8 convert_multiply_fusion
  (145 shorter events, 46.2 us)
Async XLA Ops:
  7.2 14.3 %copy-start = (bf16[256,2048]{1,0:T(8,128)(2,1)S(1)}, bf16[256,2048]{1,0:T(8,128)(2,1)}, u32[]{:S(2)}) copy-start(bf16[256,2048]{1,0:T(8,128)(2,1)} %param.5) | copy-start | bytes 3145732
  7.2 56.9 %all-reduce.5.cloned.1.call-start = ((), (), s32[]{:S(2)}) async-start(), calls=%async_computation.2 | async-start | bytes 1835008 | tf_op jit(solution)/shard_map/psum | solution.py:30
  16.1 0.9 copy-start.10
  17.1 163.9 %all-reduce.9.cloned.1.call-start = ((), (), s32[]{:S(2)}) async-start(), calls=%async_computation.4 | async-start | bytes 7340032 | tf_op jit(solution)/shard_map/psum | solution.py:41
  28.4 265.3 %all-reduce.7.cloned.1.call-start = ((), (), s32[]{:S(2)}) async-start(), calls=%async_computation.3 | async-start | bytes 6422528 | tf_op jit(solution)/shard_map/psum | solution.py:44
  64.1 5.3 copy-start.2
  68.1 4.3 copy-start.12
  70.0 1.7 copy-start.7
  71.7 559.7 %all-gather.3.cloned.1.call-start = ((), (), s32[]{:S(2)}) async-start(), calls=%async_computation.5 | async-start | bytes 8650752 | tf_op jit(solution)/shard_map/all_gather | solution.py:57
  72.3 596.1 %reduce-scatter.3.cloned.1.call-start = ((), (), s32[]{:S(2)}) async-start(), calls=%async_computation.6 | async-start | bytes 2621440 | tf_op jit(solution)/shard_map/reduce_scatter | solution.py:64
  293.7 5.0 copy-start.4
  300.9 1.7 copy-start.6
  327.4 0.7 copy-start.9
  446.0 34.1 %copy-start.13 = (s32[7]{0:T(128)S(1)}, s32[7]{0:T(128)}, u32[]{:S(2)}) copy-start(s32[7]{0:T(128)} %get-tuple-element.76) | copy-start | bytes 88
  504.9 72.6 %copy-start.5 = (f32[896,896]{1,0:T(8,128)S(1)}, f32[896,896]{1,0:T(8,128)}, u32[]{:S(2)}) copy-start(f32[896,896]{1,0:T(8,128)} %get-tuple-element.131) | copy-start | bytes 9633796
  575.7 4.3 copy-start.8
  577.5 7.3 slice-start
  581.1 3.8 slice-start.1
  622.7 1.2 copy-start.1
  622.7 1.5 copy-start.3
  631.3 7.7 copy-start.11
  639.0 85.5 %all-gather.5.cloned.1.call-start = ((), (), s32[]{:S(2)}) async-start(), calls=%async_computation.7 | async-start | bytes 8650752 | tf_op jit(solution)/shard_map/all_gather | solution.py:68
  670.2 108.2 %reduce-scatter.5.cloned.1.call-start = ((), (), s32[]{:S(2)}) async-start(), calls=%async_computation.8 | async-start | bytes 5242880 | tf_op jit(solution)/shard_map/reduce_scatter | solution.py:73
Sparse Core Ops, SparseCore 0:
  17.2 46.8 all-reduce.4
  67.4 113.4 all-reduce.8
  184.4 109.2 all-reduce.6
  295.8 53.2 all-gather.2
  639.1 29.1 reduce-scatter.2
  671.3 53.1 all-gather.4
  732.5 45.8 reduce-scatter.4
where the time goes:
time: 794 us; the launch traced here: 788 us
  waiting for transfers between devices  381 us (48%)
  other arithmetic  254 us (32%)
  matrix products  82.4 us (10%)
  local copies, waits for them, and re-layouts  42.1 us (5%)
  between operations  28.4 us (4%)
    another operation x27, other arithmetic, shards(): chol_lower = jnp.linalg.cholesky(inverse_square)  154 us
    psum x1, waiting for transfers between devices, shards(): lax.psum(jnp.concatenate(weight_parts, axis=0).astype(jnp.bfloat16), 'rows')  109 us
    psum x1, waiting for transfers between devices, shards(): inverse_square = lax.psum(jnp.concatenate(inverse_parts, axis=0), 'rows')  107 us
    another operation x3, other arithmetic, spd_solve(): lax.linalg.triangular_solve(chol_lower, forward, left_side=True, lower=Tr...  74 us
    all_gather x1, waiting for transfers between devices, shards(): lax.all_gather(own_rows, 'rows', axis=1, tiled=True)  54.3 us
    reduce_scatter x1, waiting for transfers between devices, shards(): lax.psum_scatter(gram_term.astype(jnp.bfloat16), 'mp', scatter_dimension=...  46.1 us
    psum x1, waiting for transfers between devices, shards(): columns = lax.psum(jnp.concatenate(col_pieces, axis=1), 'mp')  35.7 us
    reduce_scatter x1, waiting for transfers between devices, shards(): lax.psum_scatter(partial_value, 'mp', scatter_dimension=0, tiled=True)  29.3 us
  transfers between devices with their start and end apart: 7, of which 6 were waited for; matrix products, arithmetic and copies ran while one was open for 44% of the time, Pallas kernels for 0%

commit v1 on v0

--- a/solution.py
+++ b/solution.py
@@ -63,9 +63,16 @@
     own_rows = (
         lax.psum_scatter(partial_value, "mp", scatter_dimension=0, tiled=True) * out_scale
     ).astype(jnp.bfloat16)
+
+    def _update_counts(raw, d_out):
+        current_arr = lax.axis_size("rows")
+        view_out = jnp.stack([raw] * current_arr, axis=0)
+        w1 = lax.all_to_all(view_out, "rows", 0, 0)
+        return jnp.concatenate(w1, d_out)
+
     gram_term = lax.dot_general(
         own_rows,
-        lax.all_gather(own_rows, "rows", axis=1, tiled=True),
+        _update_counts(own_rows, 1),
         (((0,), (0,)), ((), ())),
         preferred_element_type=jnp.float32,
     )

time: 794 us -> 836 us (1.053)
  blocking collectives: 0 us -> 103 us
  waiting for transfers between devices: 381 us -> 324 us
    all_to_all x0 -> x1, blocking collectives: none -> 103 us  [_update_counts(): w1 = lax.all_to_all(view_out, 'rows', 0, 0)]
    all_gather x1 -> x0, waiting for transfers between devices: 54.3 us -> none  [shards(): lax.all_gather(own_rows, 'rows', axis=1, tiled=True)]
    another operation x21 -> x22, local copies, waits for them, and re-layouts: 24.9 us -> 25.4 us
  transfers between devices with their start and end apart: 7 -> 6, of which waited for: 6 -> 5; matrix products, arithmetic and copies ran while one was open for 44% -> 42% of each run, Pallas kernels for 0% -> 0%
where the time goes in v1:
time: 836 us; the launch traced here: 830 us
  waiting for transfers between devices  324 us (39%)
  other arithmetic  253 us (30%)
  blocking collectives  103 us (12%)
  matrix products  78.9 us (9%)
  local copies, waits for them, and re-layouts  42.7 us (5%)
  between operations  28.6 us (3%)
    another operation x27, other arithmetic, shards(): chol_lower = jnp.linalg.cholesky(inverse_square)  154 us
    psum x1, waiting for transfers between devices, shards(): lax.psum(jnp.concatenate(weight_parts, axis=0).astype(jnp.bfloat16), 'rows')  109 us
    psum x1, waiting for transfers between devices, shards(): inverse_square = lax.psum(jnp.concatenate(inverse_parts, axis=0), 'rows')  107 us
    all_to_all x1, blocking collectives, _update_counts(): w1 = lax.all_to_all(view_out, 'rows', 0, 0)  103 us
    another operation x3, other arithmetic, spd_solve(): lax.linalg.triangular_solve(chol_lower, forward, left_side=True, lower=Tr...  73.9 us
    reduce_scatter x1, waiting for transfers between devices, shards(): lax.psum_scatter(gram_term.astype(jnp.bfloat16), 'mp', scatter_dimension=...  43 us
    psum x1, waiting for transfers between devices, shards(): columns = lax.psum(jnp.concatenate(col_pieces, axis=1), 'mp')  35.5 us
    reduce_scatter x1, waiting for transfers between devices, shards(): lax.psum_scatter(partial_value, 'mp', scatter_dimension=0, tiled=True)  29.3 us
  transfers between devices with their start and end apart: 6, of which 5 were waited for; matrix products, arithmetic and copies ran while one was open for 42% of the time, Pallas kernels for 0%

profile of v1, /device:TPU:1, one launch (start us, length us, event | category | flops | bytes accessed | tf_op | source)
XLA Modules:
  0.0 830.4 jit_solution(15073076830216419069)
XLA Ops:
  13.6 1.8 constant_dynamic-slice_fusion.1
  28.6 35.5 %all-reduce.5.cloned.1.call-done = f32[256,896]{0,1:T(8,128)} async-done(((f32[256,896]{0,1:T(8,128)}), f32[256,896]{0,1:T(8,128)}) %all-reduce.5.cloned.1.call-update) | async-done | bytes 917520 | tf_op jit(solution)/shard_map/psum | solution.py:30
  64.2 1.3 multiply_dynamic-update-slice_fusion.6
  65.5 1.4 multiply_dynamic-update-slice_fusion.5
  66.8 1.4 multiply_dynamic-update-slice_fusion.4
  70.1 1.7 copy-done.7
  72.6 108.5 %all-reduce.9.cloned.1.call-done = bf16[896,2048]{1,0:T(8,128)(2,1)} async-done(((bf16[896,2048]{1,0:T(8,128)(2,1)}), bf16[896,2048]{1,0:T(8,128)(2,1)}) %all-reduce.9.cloned.1.call-update) | async-done | bytes 3670032 | tf_op jit(solution)/shard_map/psum | solution.py:41
  181.1 6.0 convert_element_type.111
  187.1 106.7 %all-reduce.7.cloned.1.call-done = f32[896,896]{0,1:T(8,128)} async-done(((f32[896,896]{0,1:T(8,128)}), f32[896,896]{0,1:T(8,128)}) %all-reduce.7.cloned.1.call-update) | async-done | bytes 3211280 | tf_op jit(solution)/shard_map/psum | solution.py:44
  293.8 5.0 copy.30
  298.8 2.2 fusion.16
  301.1 1.7 copy-done.6
  302.8 11.7 %cholesky.195 = f32[128,128]{1,0:T(8,128)S(1)} custom-call(f32[128,128]{1,0:T(8,128)S(1)} %cholesky.502), custom_call_target="Cholesky" | custom-call | tf_op jit(solution)/shard_map/jit(cholesky)/cholesky | solution.py:45
  314.8 9.8 %custom-call.56 = f32[1,128,128]{1,2,0:T(8,128)S(1)} custom-call(f32[1,128,128]{2,1,0:T(8,128)S(1)} %get-tuple-element.55), custom_call_target="InvertDiagBlocksLowerTriangular" | custom-call | tf_op jit(solution)/shard_map/jit(cholesky)/cholesky | solution.py:45
  324.6 1.5 constant_dynamic-update-slice_fusion.28
  326.0 1.5 convolution_subtract_fusion.9
  328.3 11.7 %cholesky.216 = f32[128,128]{1,0:T(8,128)S(1)} custom-call(f32[128,128]{1,0:T(8,128)S(1)} %cholesky.506), custom_call_target="Cholesky" | custom-call | tf_op jit(solution)/shard_map/jit(cholesky)/cholesky | solution.py:45
  340.7 10.0 %custom-call.57 = f32[1,128,128]{1,2,0:T(8,128)S(1)} custom-call(f32[1,128,128]{2,1,0:T(8,128)S(1)} %get-tuple-element.52), custom_call_target="InvertDiagBlocksLowerTriangular" | custom-call | tf_op jit(solution)/shard_map/jit(cholesky)/cholesky | solution.py:45
  350.7 1.4 convolution_dynamic-update-slice_fusion.1
  352.1 1.7 convolution_subtract_fusion.10
  354.3 13.2 %cholesky.411 = f32[128,128]{1,0:T(8,128)} custom-call(f32[128,128]{1,0:T(8,128)} %cholesky.511), custom_call_target="Cholesky" | custom-call | tf_op jit(solution)/shard_map/jit(cholesky)/cholesky | solution.py:45
  367.5 1.5 select_reduce_fusion.4
  369.0 11.3 %custom-call.58 = f32[1,128,128]{1,2,0:T(8,128)} custom-call(f32[1,128,128]{2,1,0:T(8,128)} %get-tuple-element.49), custom_call_target="InvertDiagBlocksLowerTriangular" | custom-call | tf_op jit(solution)/shard_map/jit(cholesky)/cholesky | solution.py:45
  381.5 1.7 convolution_subtract_fusion.11
  383.9 12.9 %cholesky.430 = f32[128,128]{1,0:T(8,128)S(1)} custom-call(f32[128,128]{1,0:T(8,128)} %cholesky.516), custom_call_target="Cholesky" | custom-call | tf_op jit(solution)/shard_map/jit(cholesky)/cholesky | solution.py:45
  397.4 10.6 %custom-call.59 = f32[1,128,128]{1,2,0:T(8,128)S(1)} custom-call(f32[1,128,128]{2,1,0:T(8,128)} %get-tuple-element.46), custom_call_target="InvertDiagBlocksLowerTriangular" | custom-call | tf_op jit(solution)/shard_map/jit(cholesky)/cholesky | solution.py:45
  408.4 1.7 convolution_subtract_fusion.12
  410.1 11.7 %cholesky.449 = f32[128,128]{1,0:T(8,128)S(1)} custom-call(f32[128,128]{1,0:T(8,128)S(1)} %cholesky.521), custom_call_target="Cholesky" | custom-call | tf_op jit(solution)/shard_map/jit(cholesky)/cholesky | solution.py:45
  422.4 9.8 %custom-call.60 = f32[1,128,128]{1,2,0:T(8,128)S(1)} custom-call(f32[1,128,128]{2,1,0:T(8,128)S(1)} %get-tuple-element.43), custom_call_target="InvertDiagBlocksLowerTriangular" | custom-call | tf_op jit(solution)/shard_map/jit(cholesky)/cholesky | solution.py:45
  432.5 1.6 convolution_subtract_fusion.13
  434.1 11.9 %cholesky.469 = f32[128,128]{1,0:T(8,128)S(1)} custom-call(f32[128,128]{1,0:T(8,128)S(1)} %cholesky.526), custom_call_target="Cholesky" | custom-call | tf_op jit(solution)/shard_map/jit(cholesky)/cholesky | solution.py:45
  446.0 9.8 %custom-call.61 = f32[1,128,128]{1,2,0:T(8,128)S(1)} custom-call(f32[1,128,128]{2,1,0:T(8,128)S(1)} %get-tuple-element.40), custom_call_target="InvertDiagBlocksLowerTriangular" | custom-call | tf_op jit(solution)/shard_map/jit(cholesky)/cholesky | solution.py:45
  456.0 1.3 convolution_subtract_fusion.14
  458.1 11.7 %cholesky.487 = f32[128,128]{1,0:T(8,128)S(1)} custom-call(f32[128,128]{1,0:T(8,128)S(1)} %convolution_subtract_fusion.14), custom_call_target="Cholesky" | custom-call | tf_op jit(solution)/shard_map/jit(cholesky)/cholesky | solution.py:45
  473.7 1.4 compare_reduce_fusion.3
  478.3 2.0 select_select_fusion
  480.3 24.5 %while.1 = (s32[]{:T(128)}, f32[896,896]{1,0:T(8,128)}, s32[7,2]{0,1:T(2,128)S(1)}, f32[7,128,128]{2,1,0:T(8,128)}, s32[]{:T(128)}) while((s32[]{:T(128)}, f32[896,896]{1,0:T(8,128)}, s32[7,2]{0,1:T(2,128)S(1)}, f32[7,128,128]{2,1,0:T(8,128)}, s32[]{:T(128)}) %tuple.62), condition=%wide.while_cond, body=%wide.while_body.sunk | while | flops 2 | bytes 132705 | solution.py:11
  480.9 2.9 bitcast_dynamic-update-slice_fusion.2
  484.4 2.9 bitcast_dynamic-update-slice_fusion.2
  487.9 2.9 bitcast_dynamic-update-slice_fusion.2
  491.4 2.9 bitcast_dynamic-update-slice_fusion.2
  494.9 2.9 bitcast_dynamic-update-slice_fusion.2
  498.5 2.9 bitcast_dynamic-update-slice_fusion.2
  502.0 2.8 bitcast_dynamic-update-slice_fusion.2
  504.8 70.7 %custom-call.62 = f32[7,128,128]{1,2,0:T(8,128)} custom-call(f32[7,128,128]{2,1,0:T(8,128)} %get-tuple-element.9), custom_call_target="InvertDiagBlocksLowerTriangular" | custom-call | tf_op jit(solution)/shard_map/triangular_solve | solution.py:11
  575.6 1.8 constant_dynamic-update-slice_fusion.4
  577.4 2.4 convolution_subtract_fusion.8
  580.9 2.6 convolution_subtract_fusion.6
  584.7 2.0 fusion.34
  587.9 2.4 fusion.40
  591.4 3.3 convolution_subtract_fusion.5
  595.8 3.4 convolution_subtract_fusion.2
  603.4 1.3 convolution_subtract_fusion.4
  605.9 2.1 fusion.31
  609.0 2.3 fusion.37
  612.8 3.1 convolution_subtract_fusion.3
  617.4 3.8 convolution_subtract_fusion.1
  624.1 7.1 fusion.30
  631.2 7.6 convolution_bitcast_fusion
  638.9 29.3 %reduce-scatter.3.cloned.1.call-done = f32[512,256]{0,1:T(8,128)} async-done(((f32[2048,256]{0,1:T(8,128)}), f32[512,256]{0,1:T(8,128)}) %reduce-scatter.3.cloned.1.call-update) | async-done | bytes 524304 | tf_op jit(solution)/shard_map/reduce_scatter | solution.py:64
  670.3 103.0 %all_to_all.5 = bf16[32,512,256]{1,2,0:T(8,128)(2,1)S(1)} all-to-all(bf16[32,512,256]{1,2,0:T(8,128)(2,1)S(1)} %stack.2), channel_id=1, replica_groups=mesh['rows'=32,'mp'=4] {'rows'}, dimensions={0} | all-to-all | bytes 16777216 | tf_op jit(solution)/shard_map/all_to_all | solution.py:70
  773.3 4.3 convolution_convert_fusion
  777.6 43.0 %reduce-scatter.5.cloned.1.call-done = bf16[256,2048]{1,0:T(8,128)(2,1)} async-done(((bf16[256,8192]{1,0:T(8,128)(2,1)}), bf16[256,2048]{1,0:T(8,128)(2,1)}) %reduce-scatter.5.cloned.1.call-update) | async-done | bytes 1048592 | tf_op jit(solution)/shard_map/reduce_scatter | solution.py:80
  820.6 2.8 convert_multiply_fusion
  (144 shorter events, 46.6 us)
Async XLA Ops:
  7.2 14.5 %copy-start = (bf16[256,2048]{1,0:T(8,128)(2,1)S(1)}, bf16[256,2048]{1,0:T(8,128)(2,1)}, u32[]{:S(2)}) copy-start(bf16[256,2048]{1,0:T(8,128)(2,1)} %param.5) | copy-start | bytes 3145732
  7.2 57.0 %all-reduce.5.cloned.1.call-start = ((), (), s32[]{:S(2)}) async-start(), calls=%async_computation.3 | async-start | bytes 1835008 | tf_op jit(solution)/shard_map/psum | solution.py:30
  16.2 0.9 copy-start.10
  17.2 163.9 %all-reduce.9.cloned.1.call-start = ((), (), s32[]{:S(2)}) async-start(), calls=%async_computation.5 | async-start | bytes 7340032 | tf_op jit(solution)/shard_map/psum | solution.py:41
  28.6 265.2 %all-reduce.7.cloned.1.call-start = ((), (), s32[]{:S(2)}) async-start(), calls=%async_computation.4 | async-start | bytes 6422528 | tf_op jit(solution)/shard_map/psum | solution.py:44
  64.2 5.3 copy-start.2
  68.2 4.3 copy-start.12
  70.1 1.7 copy-start.7
  71.8 559.4 %all-gather.2.cloned.1.call-start = ((), (), s32[]{:S(2)}) async-start(), calls=%async_computation.6 | async-start | bytes 8650752 | tf_op jit(solution)/shard_map/all_gather | solution.py:57
  72.4 595.8 %reduce-scatter.3.cloned.1.call-start = ((), (), s32[]{:S(2)}) async-start(), calls=%async_computation.7 | async-start | bytes 2621440 | tf_op jit(solution)/shard_map/reduce_scatter | solution.py:64
  293.8 5.0 copy-start.4
  301.1 1.7 copy-start.6
  327.5 0.7 copy-start.9
  446.0 34.3 %copy-start.13 = (s32[7]{0:T(128)S(1)}, s32[7]{0:T(128)}, u32[]{:S(2)}) copy-start(s32[7]{0:T(128)} %get-tuple-element.76) | copy-start | bytes 88
  504.8 72.6 %copy-start.5 = (f32[896,896]{1,0:T(8,128)S(1)}, f32[896,896]{1,0:T(8,128)}, u32[]{:S(2)}) copy-start(f32[896,896]{1,0:T(8,128)} %get-tuple-element.130) | copy-start | bytes 9633796
  575.5 4.3 copy-start.8
  577.4 7.3 slice-start
  580.9 3.8 slice-start.1
  622.6 1.2 copy-start.1
  622.6 1.5 copy-start.3
  631.2 7.7 copy-start.11
  638.9 181.7 %reduce-scatter.5.cloned.1.call-start = ((), (), s32[]{:S(2)}) async-start(), calls=%async_computation.8 | async-start | bytes 5242880 | tf_op jit(solution)/shard_map/reduce_scatter | solution.py:80
Sparse Core Ops, SparseCore 0:
  17.3 46.8 all-reduce.4
  67.6 113.4 all-reduce.8
  184.5 109.2 all-reduce.6
  295.9 53.2 all-gather.1
  639.0 29.1 reduce-scatter.2
  777.7 42.8 reduce-scatter.4
